TPU v7x, 32 devices: a whole 2x2x4 slice. The times are simulated.
32 devices in a mesh: dp: 8 (over y, x, core), expert: 4 (over z).
Axes of the slice: x: 2, y: 2, z: 4, core: 2. Of those that a mesh axis runs over, the one named last changes fastest.
Arguments:
- tokens: bfloat16 [512, 2048], P(('dp', 'expert')), may hold values from -6 to 6
- out_grad: bfloat16 [512, 2048], P(('dp', 'expert')), may hold values from -6 to 6
- gate_weights: bfloat16 [512, 2], P(('dp', 'expert')), may hold values from 0.049804688 to 1
- expert_ids: int32 [512, 2], P(('dp', 'expert')), may hold values from 0 to 3, all different within a row; in each aligned block of 16 rows (0 to 15, 16 to 31, ...) at most 10 rows name the same one
- swapped: int32 [4], replicated, may hold values from 0 to 1, as said below
- up_weight: bfloat16 [4, 2048, 384], P('expert'), may hold values from -0.125 to 0.125
- down_weight: bfloat16 [4, 384, 2048], P('expert'), may hold values from -0.3125 to 0.3125
Outputs:
- layer_out: bfloat16 [512, 2048], P(('dp', 'expert'))
- token_grad: bfloat16 [512, 2048], P(('dp', 'expert'))
- up_grad: float32 [4, 2048, 384], P('expert', 'dp')
- down_grad: float32 [4, 384, 2048], P('expert', 'dp')
Inputs may be any that keep to these rules, and one draw needn't show every extreme that they name: swapped[s] equals swapped[(s + 2) mod 4]; swapped[0] is 1. `expert_ids`: A token's 2 experts differ; at most 10 of the tokens of one device name one expert, and that many in some device.
All inputs are finite; a program needn't handle non-finite values.
Results may differ from a plain program's by a relative error of at most 0.023.
Values may be sent and summed in bfloat16 or wider, within the bound.
A program may use at most 64 MiB of HBM per device.

v0:
```python
import jax
import jax.numpy as jnp
from jax import lax
from jax.sharding import PartitionSpec as P

BF = jnp.bfloat16
F32 = jnp.float32


def on_device(tokens, out_grad, gate_weights, expert_ids, swapped, up_weight, down_weight):
    owners = lax.axis_size("expert")
    mine = lax.axis_index("expert")
    width = tokens.shape[1]
    lanes = jnp.arange(128, dtype=jnp.int32)
    hit = expert_ids[:, :, None] == lanes[None, None, :]
    gates = jnp.sum(jnp.where(hit, gate_weights.astype(F32)[:, :, None], 0.0), axis=1).astype(BF)
    packed = jnp.concatenate([tokens, out_grad, gates], axis=1)
    full = lax.all_gather(packed, "expert", axis=0, tiled=True)
    x, og, gates = (full[:, :width], full[:, width : 2 * width], full[:, 2 * width :])
    gates = gates.astype(F32)
    flag = lax.dynamic_slice_in_dim(swapped, mine, 1, 0)[0] == 1
    held = jnp.where(flag, (mine + owners // 2) % owners, mine)

    def column(e):
        return jnp.sum(jnp.where(lanes[None, :] == e, gates, 0.0), axis=1, keepdims=True)

    gate = column(mine)
    up, down = (up_weight[0], down_weight[0])
    dy = (gate * og.astype(F32)).astype(BF)
    hidden = jnp.dot(x, up, preferred_element_type=F32)
    d_active = lax.dot_general(dy, down, (((1,), (1,)), ((), ())), preferred_element_type=F32)
    sigma = jax.nn.sigmoid(hidden)
    active = jnp.where(gate > 0, hidden * sigma, 0.0).astype(BF)
    d_hidden = (d_active * sigma * (1.0 + hidden * (1.0 - sigma))).astype(BF)
    other = lax.ppermute(
        jnp.concatenate([active, d_hidden], axis=1),
        "expert",
        [(i, (i + owners // 2) % owners) for i in range(owners)],
    )
    y = jnp.dot(active, down, preferred_element_type=F32).astype(BF).astype(F32)
    dx = lax.dot_general(d_hidden, up, (((1,), (1,)), ((), ())), preferred_element_type=F32)
    back = jnp.concatenate([(gate * y).astype(BF), dx.astype(BF)], axis=1)
    back = lax.psum_scatter(back, "expert", scatter_dimension=0, tiled=True)
    fw = active.shape[1]
    act_h = jnp.where(flag, other[:, :fw], active)
    dh_h = jnp.where(flag, other[:, fw:], d_hidden)
    dy_h = (column(held) * og.astype(F32)).astype(BF)
    over = (((0,), (0,)), ((), ()))
    part_up = lax.dot_general(x, dh_h, over, preferred_element_type=F32).astype(BF)
    part_down = lax.dot_general(act_h, dy_h, over, preferred_element_type=F32).astype(BF)
    sum_up = lax.psum_scatter(part_up, "dp", scatter_dimension=0, tiled=True).astype(F32)
    sum_down = lax.psum_scatter(part_down, "dp", scatter_dimension=0, tiled=True).astype(F32)
    return (back[:, :width], back[:, width:], sum_up[None], sum_down[None])


def solution(mesh):
    rows = P(("dp", "expert"), None)
    in_specs = (rows, rows, rows, rows, P(), P("expert", None, None), P("expert", None, None))
    out_specs = (rows, rows, P("expert", "dp", None), P("expert", "dp", None))
    return jax.shard_map(
        on_device, mesh=mesh, in_specs=in_specs, out_specs=out_specs, check_vma=False
    )
```

profile of v0, /device:TPU:0, one launch (start us, length us, event | category | flops | bytes accessed | tf_op | source)
XLA Modules:
  0.0 145.8 jit_solution(18337395478298540508)
XLA Ops:
  7.2 0.0 copy-start
  7.2 0.0 reduce-scatter.4.cloned.1.call-start
  7.2 1.3 dynamic_slice.3
  9.2 0.0 copy-start.1
  9.3 0.8 convert_element_type.45
  10.0 0.8 select_reduce_fusion
  10.8 0.9 pad_maximum_fusion.1
  11.7 17.5 %all_gather.3 = bf16[64,4224]{1,0:T(8,128)(2,1)S(1)} all-gather(bf16[16,4224]{1,0:T(8,128)(2,1)S(1)} %pad_maximum_fusion.1), channel_id=1, replica_groups=mesh['dp'=8,'expert'=4] {'expert'}, dimensions={0}, use_global_device_ids=true | all-gather | bytes 675840 | tf_op jit(solution)/shard_map/all_gather | solution.py:18
  29.2 0.1 fusion.31
  29.3 0.0 copy-done
  29.3 0.4 select_convert_fusion
  29.7 0.0 copy-done.1
  29.7 0.6 fusion.15
  30.3 0.4 fusion.2
  30.8 0.6 convolution_convert_fusion.2
  31.4 0.8 pad_maximum_fusion
  32.2 0.0 reduce-scatter.4.cloned.1.call-update
  32.2 0.0 reduce-scatter.8.cloned.1.call-start
  32.3 0.8 collective-permute-start
  33.1 4.8 %collective-permute-done = bf16[64,768]{1,0:T(8,128)(2,1)S(1)} collective-permute-done((bf16[64,768]{1,0:T(8,128)(2,1)S(1)}, bf16[64,768]{1,0:T(8,128)(2,1)S(1)}, u32[]{:S(2)}, u32[]{:S(2)}) %collective-permute-start) | collective-permute-done | bytes 98336 | tf_op jit(solution)/shard_map/ppermute | solution.py:35
  37.9 1.8 %convolution_convert_fusion = bf16[384,2048]{1,0:T(8,128)(2,1)} fusion(f32[64]{0:T(128)S(1)} %get-tuple-element.4, bf16[64,4224]{1,0:T(8,128)(2,1)S(1)} %all_gather.3, bf16[64,384]{1,0:T(8,128)(2,1)S(1)} %get-tuple-element.8, bf16[64,768]{1,0:T(8,128)(2,1)S(1)} %collective-permute-done, pred[]{:T(512)} %bitcast.2), kind=kOutput, calls=%fused_computation | convolution fusion | flops 101867520 | bytes 1933825 | tf_op jit(solution)/shard_map/dot_general | solution.py:50
  39.7 0.0 reduce-scatter.8.cloned.1.call-update
  39.7 0.0 reduce-scatter.6.cloned.1.call-start
  39.7 1.8 %convolution_convert_fusion.1 = bf16[2048,384]{1,0:T(8,128)(2,1)} fusion(bf16[64,4224]{1,0:T(8,128)(2,1)S(1)} %all_gather.3, bf16[64,384]{1,0:T(8,128)(2,1)S(1)} %fusion.15, bf16[64,768]{1,0:T(8,128)(2,1)S(1)} %collective-permute-done, pred[]{:T(512)} %bitcast.2), kind=kOutput, calls=%fused_computation.1 | convolution fusion | flops 101474304 | bytes 1933313 | tf_op jit(solution)/shard_map/dot_general | solution.py:49
  41.5 0.0 reduce-scatter.6.cloned.1.call-update
  41.5 14.2 %reduce-scatter.4.cloned.1.call-done = bf16[16,4096]{1,0:T(8,128)(2,1)} async-done(((bf16[64,4096]{1,0:T(8,128)(2,1)}), bf16[16,4096]{1,0:T(8,128)(2,1)}) %reduce-scatter.4.cloned.1.call-update) | async-done | bytes 131088 | tf_op jit(solution)/shard_map/reduce_scatter | solution.py:43
  55.8 1.5 %fusion.32 = (bf16[16,2048]{1,0:T(8,128)(2,1)}, bf16[16,2048]{1,0:T(8,128)(2,1)}) fusion(bf16[16,4096]{1,0:T(8,128)(2,1)} %reduce-scatter.4.cloned.1.call-done), kind=kLoop, calls=%fused_computation.46 | loop fusion | bytes 262144 | tf_op jit(solution)/shard_map/slice | solution.py:53
  57.3 38.5 %reduce-scatter.8.cloned.1.call-done = bf16[48,2048]{1,0:T(8,128)(2,1)} async-done(((bf16[384,2048]{1,0:T(8,128)(2,1)}), bf16[48,2048]{1,0:T(8,128)(2,1)}) %reduce-scatter.8.cloned.1.call-update) | async-done | bytes 196624 | tf_op jit(solution)/shard_map/reduce_scatter | solution.py:52
  95.8 1.7 %bitcast_convert_fusion = f32[1,48,2048]{2,1,0:T(8,128)} fusion(bf16[48,2048]{1,0:T(8,128)(2,1)} %reduce-scatter.8.cloned.1.call-done), kind=kLoop, calls=%fused_computation.27 | loop fusion | flops 98304 | bytes 589824 | tf_op jit(solution)/shard_map/broadcast_in_dim | solution.py:53
  97.5 40.1 %reduce-scatter.6.cloned.1.call-done = bf16[256,384]{1,0:T(8,128)(2,1)} async-done(((bf16[2048,384]{1,0:T(8,128)(2,1)}), bf16[256,384]{1,0:T(8,128)(2,1)}) %reduce-scatter.6.cloned.1.call-update) | async-done | bytes 196624 | tf_op jit(solution)/shard_map/reduce_scatter | solution.py:51
  137.6 1.7 %bitcast_convert_fusion.1 = f32[1,256,384]{2,1,0:T(8,128)} fusion(bf16[256,384]{1,0:T(8,128)(2,1)} %reduce-scatter.6.cloned.1.call-done), kind=kLoop, calls=%fused_computation.28 | loop fusion | flops 98304 | bytes 589824 | tf_op jit(solution)/shard_map/broadcast_in_dim | solution.py:53
  (3 shorter events, 0.0 us)
Async XLA Ops:
  7.2 22.2 %copy-start = (bf16[1,2048,384]{2,1,0:T(8,128)(2,1)S(1)}, bf16[1,2048,384]{2,1,0:T(8,128)(2,1)}, u32[]{:S(2)}) copy-start(bf16[1,2048,384]{2,1,0:T(8,128)(2,1)} %param.12) | copy-start | bytes 4718596
  7.2 48.6 %reduce-scatter.4.cloned.1.call-start = ((), (), s32[]{:S(2)}) async-start(), calls=%async_computation.3 | async-start | bytes 655360 | tf_op jit(solution)/shard_map/reduce_scatter | solution.py:43
  9.2 20.5 %copy-start.1 = (bf16[1,384,2048]{2,1,0:T(8,128)(2,1)S(1)}, bf16[1,384,2048]{2,1,0:T(8,128)(2,1)}, u32[]{:S(2)}) copy-start(bf16[1,384,2048]{2,1,0:T(8,128)(2,1)} %param.13) | copy-start | bytes 4718596
  32.2 63.6 %reduce-scatter.8.cloned.1.call-start = ((), (), s32[]{:S(2)}) async-start(), calls=%async_computation.5 | async-start | bytes 1769472 | tf_op jit(solution)/shard_map/reduce_scatter | solution.py:52
  32.3 5.6 %collective-permute-start = (bf16[64,768]{1,0:T(8,128)(2,1)S(1)}, bf16[64,768]{1,0:T(8,128)(2,1)S(1)}, u32[]{:S(2)}, u32[]{:S(2)}) collective-permute-start(bf16[64,768]{1,0:T(8,128)(2,1)S(1)} %pad_maximum_fusion.2), channel_id=1, source_target_pairs={{0,2},{1,3},{2,0},{3,1},{4,6},{5,7},{6,4},{7,5},{8,10},{9,11},{10,... | collective-permute-start | bytes 294920 | tf_op jit(solution)/shard_map/ppermute | solution.py:35
  39.7 97.9 %reduce-scatter.6.cloned.1.call-start = ((), (), s32[]{:S(2)}) async-start(), calls=%async_computation.4 | async-start | bytes 1769472 | tf_op jit(solution)/shard_map/reduce_scatter | solution.py:51
Sparse Core Ops, SparseCore 0:
  32.3 23.3 reduce-scatter.3
  59.1 36.7 reduce-scatter.7
  99.1 38.4 reduce-scatter.5
where the time goes:
time: 146 us
  waiting for transfers between devices  97.7 us (67%)
  blocking collectives  17.5 us (12%)
  between operations  14.5 us (10%)
  other arithmetic  6.76 us (5%)
  matrix products  5.55 us (4%)
  local copies, waits for them, and re-layouts  2.89 us (2%)
    reduce_scatter x1, waiting for transfers between devices, on_device(): lax.psum_scatter(part_up, 'dp', scatter_dimension=0, tiled=True).astype(F32)  40.1 us
    reduce_scatter x1, waiting for transfers between devices, on_device(): lax.psum_scatter(part_down, 'dp', scatter_dimension=0, tiled=True)  38.5 us
    all_gather x1, blocking collectives, on_device(): full = lax.all_gather(packed, 'expert', axis=0, tiled=True)  17.5 us
    reduce_scatter x1, waiting for transfers between devices, on_device(): back = lax.psum_scatter(back, 'expert', scatter_dimension=0, tiled=True)  14.2 us
    ppermute x1, waiting for transfers between devices, on_device(): lax.ppermute(jnp.concatenate([active, d_hidden], axis=1), 'expert', [(i,...  4.77 us
    broadcast_in_dim x2, other arithmetic, on_device(): return (back[:, :width], back[:, width:], sum_up[None], sum_down[None])  3.4 us
  transfers between devices with their start and end apart: 4, of which 4 were waited for; matrix products, arithmetic and copies ran while one was open for 5% of the time, Pallas kernels for 0%

commit v1 on v0

--- a/solution.py
+++ b/solution.py
@@ -2,6 +2,7 @@
 import jax.numpy as jnp
 from jax import lax
 from jax.sharding import PartitionSpec as P
+from jax.lax import axis_index, axis_size, ppermute
 
 BF = jnp.bfloat16
 F32 = jnp.float32
@@ -15,7 +16,22 @@
     hit = expert_ids[:, :, None] == lanes[None, None, :]
     gates = jnp.sum(jnp.where(hit, gate_weights.astype(F32)[:, :, None], 0.0), axis=1).astype(BF)
     packed = jnp.concatenate([tokens, out_grad, gates], axis=1)
-    full = lax.all_gather(packed, "expert", axis=0, tiled=True)
+    u1, block_last, s_next = (axis_size("expert"), axis_index("expert"), packed.shape[0])
+    table = tuple((c * u1 if tick == 0 else c for tick, c in enumerate(packed.shape)))
+    then = mid_arr = packed
+    full = lax.dynamic_update_slice_in_dim(
+        jnp.zeros(table, packed.dtype), packed, block_last * s_next, axis=0
+    )
+    for j0 in range(1, u1 // 2 + 1):
+        then = ppermute(then, "expert", tuple(((tick, (tick + 1) % u1) for tick in range(u1))))
+        full = lax.dynamic_update_slice_in_dim(full, then, (block_last - j0) % u1 * s_next, axis=0)
+        if 2 * j0 < u1:
+            mid_arr = ppermute(
+                mid_arr, "expert", tuple(((tick, (tick - 1) % u1) for tick in range(u1)))
+            )
+            full = lax.dynamic_update_slice_in_dim(
+                full, mid_arr, (block_last + j0) % u1 * s_next, axis=0
+            )
     x, og, gates = (full[:, :width], full[:, width : 2 * width], full[:, 2 * width :])
     gates = gates.astype(F32)
     flag = lax.dynamic_slice_in_dim(swapped, mine, 1, 0)[0] == 1

time: 146 us -> 141 us (0.966)
  blocking collectives: 17.5 us -> 0 us
  waiting for transfers between devices: 97.7 us -> 104 us
  starting transfers between devices: 0.93 us -> 6.07 us
    all_gather x1 -> x0, blocking collectives: 17.5 us -> none  [on_device(): full = lax.all_gather(packed, 'expert', axis=0, tiled=True)]
    ppermute x0 -> x3, waiting for transfers between devices: none -> 9.21 us  [the longest x2 7.75 us: on_device(): ppermute(then, 'expert', tuple(((tick, (tick + 1) % u1) for tick in range...]
    ppermute x0 -> x3, starting transfers between devices: none -> 5.17 us  [the longest x2 3.08 us: on_device(): ppermute(then, 'expert', tuple(((tick, (tick + 1) % u1) for tick in range...]
    reduce_scatter x1, waiting for transfers between devices: 14.2 us -> 11.7 us  [on_device(): back = lax.psum_scatter(back, 'expert', scatter_dimension=0, tiled=True)]
  transfers between devices with their start and end apart: 4 -> 7, of which waited for: 4 -> 7; matrix products, arithmetic and copies ran while one was open for 5% -> 6% of each run, Pallas kernels for 0% -> 0%
where the time goes in v1:
time: 141 us; the launch traced here: 140 us
  waiting for transfers between devices  104 us (74%)
  between operations  14.5 us (10%)
  other arithmetic  6.78 us (5%)
  starting transfers between devices  6.07 us (4%)
  matrix products  5.59 us (4%)
  local copies, waits for them, and re-layouts  2.87 us (2%)
    reduce_scatter x1, waiting for transfers between devices, on_device(): lax.psum_scatter(part_up, 'dp', scatter_dimension=0, tiled=True).astype(F32)  40.1 us
    reduce_scatter x1, waiting for transfers between devices, on_device(): lax.psum_scatter(part_down, 'dp', scatter_dimension=0, tiled=True)  38.5 us
    reduce_scatter x1, waiting for transfers between devices, on_device(): back = lax.psum_scatter(back, 'expert', scatter_dimension=0, tiled=True)  11.7 us
    ppermute x2, waiting for transfers between devices, on_device(): ppermute(then, 'expert', tuple(((tick, (tick + 1) % u1) for tick in range...  7.75 us
    ppermute x1, waiting for transfers between devices, on_device(): lax.ppermute(jnp.concatenate([active, d_hidden], axis=1), 'expert', [(i,...  4.9 us
    broadcast_in_dim x2, other arithmetic, on_device(): return (back[:, :width], back[:, width:], sum_up[None], sum_down[None])  3.4 us
    ppermute x2, starting transfers between devices, on_device(): ppermute(then, 'expert', tuple(((tick, (tick + 1) % u1) for tick in range...  3.08 us
  transfers between devices with their start and end apart: 7, of which 7 were waited for; matrix products, arithmetic and copies ran while one was open for 6% of the time, Pallas kernels for 0%

profile of v1, /device:TPU:0, one launch (start us, length us, event | category | flops | bytes accessed | tf_op | source)
XLA Modules:
  0.0 140.2 jit_solution(7353293040393145104)
XLA Ops:
  7.2 0.0 copy-start
  7.2 0.0 reduce-scatter.4.cloned.1.call-start
  7.2 0.8 convert_element_type.45
  8.0 0.8 select_reduce_fusion
  8.8 0.9 pad_maximum_fusion.1
  9.7 3.1 %collective-permute-start = (bf16[16,4224]{1,0:T(8,128)(2,1)S(1)}, bf16[16,4224]{1,0:T(8,128)(2,1)S(1)}, u32[]{:S(2)}, u32[]{:S(2)}) collective-permute-start(bf16[16,4224]{1,0:T(8,128)(2,1)S(1)} %get-tuple-element.6), channel_id=1, source_target_pairs={{0,1},{1,2},{2,3},{3,0},{4,5},{5,6},{6,7},{7,4},{8,9},{9,10},{10,1... | collective-permute-start | bytes 405512 | tf_op jit(solution)/shard_map/ppermute | solution.py:26
  12.8 2.1 %collective-permute-start.1 = (bf16[16,4224]{1,0:T(8,128)(2,1)S(1)}, bf16[16,4224]{1,0:T(8,128)(2,1)S(1)}, u32[]{:S(2)}, u32[]{:S(2)}) collective-permute-start(bf16[16,4224]{1,0:T(8,128)(2,1)S(1)} %get-tuple-element.6), channel_id=1, source_target_pairs={{0,3},{1,0},{2,1},{3,2},{4,7},{5,4},{6,5},{7,6},{8,11},{9,8},{10,9... | collective-permute-start | bytes 405512 | tf_op jit(solution)/shard_map/ppermute | solution.py:29
  14.9 1.2 dynamic_slice.3
  16.8 2.4 %collective-permute-done = bf16[16,4224]{1,0:T(8,128)(2,1)S(1)} collective-permute-done((bf16[16,4224]{1,0:T(8,128)(2,1)S(1)}, bf16[16,4224]{1,0:T(8,128)(2,1)S(1)}, u32[]{:S(2)}, u32[]{:S(2)}) %collective-permute-start) | collective-permute-done | bytes 135200 | tf_op jit(solution)/shard_map/ppermute | solution.py:26
  19.2 1.5 %collective-permute-done.1 = bf16[16,4224]{1,0:T(8,128)(2,1)S(1)} collective-permute-done((bf16[16,4224]{1,0:T(8,128)(2,1)S(1)}, bf16[16,4224]{1,0:T(8,128)(2,1)S(1)}, u32[]{:S(2)}, u32[]{:S(2)}) %collective-permute-start.1) | collective-permute-done | bytes 135200 | tf_op jit(solution)/shard_map/ppermute | solution.py:29
  20.7 5.3 %collective-permute-done.2 = bf16[16,4224]{1,0:T(8,128)(2,1)S(1)} collective-permute-done((bf16[16,4224]{1,0:T(8,128)(2,1)S(1)}, bf16[16,4224]{1,0:T(8,128)(2,1)S(1)}, u32[]{:S(2)}, u32[]{:S(2)}) %collective-permute-start.2) | collective-permute-done | bytes 135200 | tf_op jit(solution)/shard_map/ppermute | solution.py:26
  26.1 0.1 fusion.35
  26.2 0.4 select_convert_fusion
  26.6 0.6 fusion.21
  27.2 0.4 fusion.2
  27.6 0.6 convolution_convert_fusion.2
  28.2 0.8 pad_maximum_fusion
  29.1 0.0 reduce-scatter.4.cloned.1.call-update
  29.1 0.0 reduce-scatter.8.cloned.1.call-start
  29.2 0.8 collective-permute-start.3
  29.9 4.9 %collective-permute-done.3 = bf16[64,768]{1,0:T(8,128)(2,1)S(1)} collective-permute-done((bf16[64,768]{1,0:T(8,128)(2,1)S(1)}, bf16[64,768]{1,0:T(8,128)(2,1)S(1)}, u32[]{:S(2)}, u32[]{:S(2)}) %collective-permute-start.3) | collective-permute-done | bytes 98336 | tf_op jit(solution)/shard_map/ppermute | solution.py:51
  34.8 1.8 %convolution_convert_fusion = bf16[384,2048]{1,0:T(8,128)(2,1)} fusion(f32[64]{0:T(128)S(1)} %get-tuple-element.4, bf16[64,4224]{1,0:T(8,128)(2,1)S(1)} %constant_dynamic-update-slice_fusion, bf16[64,384]{1,0:T(8,128)(2,1)S(1)} %get-tuple-element.10, bf16[64,768]{1,0:T(8,128)(2,1)S(1)} %collective-permute-done.3, pred[]{:T(512)} %bitcast.2), kind=kOutput, calls=%fused_computation | convolution fusion | flops 101867520 | bytes 1933825 | tf_op jit(solution)/shard_map/dot_general | solution.py:66
  36.6 0.0 reduce-scatter.8.cloned.1.call-update
  36.7 0.0 reduce-scatter.6.cloned.1.call-start
  36.7 1.8 %convolution_convert_fusion.1 = bf16[2048,384]{1,0:T(8,128)(2,1)} fusion(bf16[64,4224]{1,0:T(8,128)(2,1)S(1)} %constant_dynamic-update-slice_fusion, bf16[64,384]{1,0:T(8,128)(2,1)S(1)} %fusion.21, bf16[64,768]{1,0:T(8,128)(2,1)S(1)} %collective-permute-done.3, pred[]{:T(512)} %bitcast.2), kind=kOutput, calls=%fused_computation.1 | convolution fusion | flops 101474304 | bytes 1933313 | tf_op jit(solution)/shard_map/dot_general | solution.py:65
  38.5 0.0 reduce-scatter.6.cloned.1.call-update
  38.5 11.7 %reduce-scatter.4.cloned.1.call-done = bf16[16,4096]{1,0:T(8,128)(2,1)} async-done(((bf16[64,4096]{1,0:T(8,128)(2,1)}), bf16[16,4096]{1,0:T(8,128)(2,1)}) %reduce-scatter.4.cloned.1.call-update) | async-done | bytes 131088 | tf_op jit(solution)/shard_map/reduce_scatter | solution.py:59
  50.2 1.5 %fusion.36 = (bf16[16,2048]{1,0:T(8,128)(2,1)}, bf16[16,2048]{1,0:T(8,128)(2,1)}) fusion(bf16[16,4096]{1,0:T(8,128)(2,1)} %reduce-scatter.4.cloned.1.call-done), kind=kLoop, calls=%fused_computation.50 | loop fusion | bytes 262144 | tf_op jit(solution)/shard_map/slice | solution.py:69
  51.7 38.5 %reduce-scatter.8.cloned.1.call-done = bf16[48,2048]{1,0:T(8,128)(2,1)} async-done(((bf16[384,2048]{1,0:T(8,128)(2,1)}), bf16[48,2048]{1,0:T(8,128)(2,1)}) %reduce-scatter.8.cloned.1.call-update) | async-done | bytes 196624 | tf_op jit(solution)/shard_map/reduce_scatter | solution.py:68
  90.2 1.7 %bitcast_convert_fusion = f32[1,48,2048]{2,1,0:T(8,128)} fusion(bf16[48,2048]{1,0:T(8,128)(2,1)} %reduce-scatter.8.cloned.1.call-done), kind=kLoop, calls=%fused_computation.27 | loop fusion | flops 98304 | bytes 589824 | tf_op jit(solution)/shard_map/broadcast_in_dim | solution.py:69
  91.9 40.1 %reduce-scatter.6.cloned.1.call-done = bf16[256,384]{1,0:T(8,128)(2,1)} async-done(((bf16[2048,384]{1,0:T(8,128)(2,1)}), bf16[256,384]{1,0:T(8,128)(2,1)}) %reduce-scatter.6.cloned.1.call-update) | async-done | bytes 196624 | tf_op jit(solution)/shard_map/reduce_scatter | solution.py:67
  132.0 1.7 %bitcast_convert_fusion.1 = f32[1,256,384]{2,1,0:T(8,128)} fusion(bf16[256,384]{1,0:T(8,128)(2,1)} %reduce-scatter.6.cloned.1.call-done), kind=kLoop, calls=%fused_computation.28 | loop fusion | flops 98304 | bytes 589824 | tf_op jit(solution)/shard_map/broadcast_in_dim | solution.py:69
  (11 shorter events, 0.1 us)
Async XLA Ops:
  7.2 19.0 %copy-start = (bf16[1,2048,384]{2,1,0:T(8,128)(2,1)S(1)}, bf16[1,2048,384]{2,1,0:T(8,128)(2,1)}, u32[]{:S(2)}) copy-start(bf16[1,2048,384]{2,1,0:T(8,128)(2,1)} %param.12) | copy-start | bytes 4718596
  7.2 43.0 %reduce-scatter.4.cloned.1.call-start = ((), (), s32[]{:S(2)}) async-start(), calls=%async_computation.3 | async-start | bytes 655360 | tf_op jit(solution)/shard_map/reduce_scatter | solution.py:59
  9.7 9.5 %collective-permute-start = (bf16[16,4224]{1,0:T(8,128)(2,1)S(1)}, bf16[16,4224]{1,0:T(8,128)(2,1)S(1)}, u32[]{:S(2)}, u32[]{:S(2)}) collective-permute-start(bf16[16,4224]{1,0:T(8,128)(2,1)S(1)} %get-tuple-element.6), channel_id=1, source_target_pairs={{0,1},{1,2},{2,3},{3,0},{4,5},{5,6},{6,7},{7,4},{8,9},{9,10},{10,1... | collective-permute-start | bytes 405512 | tf_op jit(solution)/shard_map/ppermute | solution.py:26
  12.8 7.9 %collective-permute-start.1 = (bf16[16,4224]{1,0:T(8,128)(2,1)S(1)}, bf16[16,4224]{1,0:T(8,128)(2,1)S(1)}, u32[]{:S(2)}, u32[]{:S(2)}) collective-permute-start(bf16[16,4224]{1,0:T(8,128)(2,1)S(1)} %get-tuple-element.6), channel_id=1, source_target_pairs={{0,3},{1,0},{2,1},{3,2},{4,7},{5,4},{6,5},{7,6},{8,11},{9,8},{10,9... | collective-permute-start | bytes 405512 | tf_op jit(solution)/shard_map/ppermute | solution.py:29
  16.8 9.8 %copy-start.1 = (bf16[1,384,2048]{2,1,0:T(8,128)(2,1)S(1)}, bf16[1,384,2048]{2,1,0:T(8,128)(2,1)}, u32[]{:S(2)}) copy-start(bf16[1,384,2048]{2,1,0:T(8,128)(2,1)} %param.13) | copy-start | bytes 4718596
  19.2 6.8 %collective-permute-start.2 = (bf16[16,4224]{1,0:T(8,128)(2,1)S(1)}, bf16[16,4224]{1,0:T(8,128)(2,1)S(1)}, u32[]{:S(2)}, u32[]{:S(2)}) collective-permute-start(bf16[16,4224]{1,0:T(8,128)(2,1)S(1)} %collective-permute-done), channel_id=1, source_target_pairs={{0,1},{1,2},{2,3},{3,0},{4,5},{5,6},{6,7},{7,4},{8,9},{9,10},{10,1... | collective-permute-start | bytes 405512 | tf_op jit(solution)/shard_map/ppermute | solution.py:26
  29.1 61.1 %reduce-scatter.8.cloned.1.call-start = ((), (), s32[]{:S(2)}) async-start(), calls=%async_computation.5 | async-start | bytes 1769472 | tf_op jit(solution)/shard_map/reduce_scatter | solution.py:68
  29.2 5.7 %collective-permute-start.3 = (bf16[64,768]{1,0:T(8,128)(2,1)S(1)}, bf16[64,768]{1,0:T(8,128)(2,1)S(1)}, u32[]{:S(2)}, u32[]{:S(2)}) collective-permute-start(bf16[64,768]{1,0:T(8,128)(2,1)S(1)} %pad_maximum_fusion.2), channel_id=1, source_target_pairs={{0,2},{1,3},{2,0},{3,1},{4,6},{5,7},{6,4},{7,5},{8,10},{9,11},{10,... | collective-permute-start | bytes 294920 | tf_op jit(solution)/shard_map/ppermute | solution.py:51
  36.7 95.3 %reduce-scatter.6.cloned.1.call-start = ((), (), s32[]{:S(2)}) async-start(), calls=%async_computation.4 | async-start | bytes 1769472 | tf_op jit(solution)/shard_map/reduce_scatter | solution.py:67
Sparse Core Ops, SparseCore 0:
  29.2 20.9 reduce-scatter.3
  53.5 36.6 reduce-scatter.7
  93.5 38.4 reduce-scatter.5
